TPU v7x, 32 devices: a whole 2x2x4 slice. The times are simulated.
32 devices in a mesh: groups: 2 (over y), expert: 2 (over x), tensor: 4 (over z), replica: 2 (over core).
Axes of the slice: x: 2, y: 2, z: 4, core: 2. Of those that a mesh axis runs over, the one named last changes fastest.
Arguments:
- tokens: bfloat16 [2048, 3072], P(('groups', 'replica'), 'tensor'), parts along dimension 0, may hold values from -6 to 6
- w_gate: bfloat16 [4, 3072, 16384], P('expert', 'replica', 'tensor'), may hold values from -0.109375 to 0.109375
- w_up: bfloat16 [4, 3072, 16384], P('expert', 'replica', 'tensor'), may hold values from -0.109375 to 0.109375
- w_down: bfloat16 [4, 16384, 3072], P('expert', 'tensor', 'replica'), may hold values from -0.0625 to 0.0625
- block_rows: int32 [4, 4, 512], P('expert', ('groups', 'replica')), parts along dimension 1, may hold values from 0 to 511, as said below
- block_gates: float32 [4, 4, 512], P('expert', ('groups', 'replica')), parts along dimension 1, may hold values from 0 to 1, as said below
- block_count: int32 [4, 4], P('expert', ('groups', 'replica')), parts along dimension 1, may hold values from 1 to 4, as said below
Outputs:
- moe_output: bfloat16 [2048, 3072], P(('groups', 'replica'), 'tensor'), parts along dimension 0
There are 2 independent parts, one for each index of `groups`. A program takes and returns all parts, laid end to end along the dimension named above; an argument that names none is the same for every part. Nothing has to cross between parts.
Inputs may be any that keep to these rules, and one draw needn't show every extreme that they name: `block_rows`: for each expert e and replica index r, the first slots of the list name the index, among the 512 tokens of replica index r, of tokens routed to e, all distinct; every such token is named so by exactly 2 experts. The rows end inside the last counted block; the remaining slots of that block and all slots past the count hold arbitrary indices. `block_gates`: positive on an expert's rows, 0 on the slots after its rows inside its last counted block, arbitrary past the count. `block_count`: for each replica index some expert has exactly 4 counted blocks; for each expert the counts over the 2 replica indices add up to at most 6, and some expert reaches that total.
All inputs are finite; a program needn't handle non-finite values.
Results may differ from a plain program's by a relative error of at most 0.013.
Values may be sent and summed in bfloat16 or wider, within the bound.
A program may use at most 448 MiB of HBM per device.

v0:
```python
import functools

import jax
import jax.numpy as jnp
from jax import lax
from jax.experimental import pallas as pl
from jax.experimental.pallas import tpu as pltpu
from jax.sharding import PartitionSpec as P

BLOCK = 128
TILE = 512
VMEM_BYTES = 48 * 1024 * 1024
MESH = pl.DeviceIdType.MESH
PAIR_BLOCKS = 6
SWAP = ((0, 1), (1, 0))


def swap_cores(x):
    return lax.ppermute(x, "replica", SWAP)


def half_of(x, axis, which):
    size = x.shape[axis] // 2
    return lax.dynamic_slice_in_dim(x, which * size, size, axis)


def dot(a, b):
    return jnp.dot(a, b, preferred_element_type=jnp.float32)


def slot_lists(block_rows, block_gates, block_count, core, token_rows):
    experts, _, slots = block_rows.shape
    blocks = slots // BLOCK
    counts = jnp.broadcast_to(block_count.astype(jnp.float32)[:, :, None], block_rows.shape)
    mine = jnp.concatenate([block_rows.astype(jnp.float32), block_gates, counts], axis=1)
    other = swap_cores(mine)
    first = jnp.where(core == 0, mine, other)
    second = jnp.where(core == 0, other, mine)
    shift = jnp.float32(token_rows)
    first_rows = first[:, 0]
    second_rows = second[:, 0] + shift
    rows = jnp.concatenate([first_rows, second_rows], axis=1).reshape(experts, 1, 2 * blocks, BLOCK)
    gates = jnp.concatenate([first[:, 1], second[:, 1]], axis=1).reshape(experts, 1, 2 * blocks, BLOCK)
    n_first = first[:, 2, :1].astype(jnp.int32)
    n_second = second[:, 2, :1].astype(jnp.int32)
    at = jnp.arange(PAIR_BLOCKS, dtype=jnp.int32)[None, :]
    source = jnp.where(at < n_first, at, blocks + at - n_first)
    source = jnp.where(at < n_first + n_second, source, -1)
    pick = source[:, :, None] == jnp.arange(2 * blocks, dtype=jnp.int32)[None, None, :]
    pick = pick[:, :, :, None]
    ids = jnp.sum(jnp.where(pick, rows, 0.0), axis=2).reshape(experts, PAIR_BLOCKS * BLOCK)
    weight = jnp.sum(jnp.where(pick, gates, 0.0), axis=2).reshape(experts, PAIR_BLOCKS * BLOCK)
    return ids.astype(jnp.int32), weight


def weight_spec(shape, e, split, which):
    if split == 2:
        tile = min(TILE, shape[2] // 2)
        per = shape[2] // 2 // tile
        return pl.BlockSpec(
            (1, shape[1], tile),
            lambda j, at: (e, 0, (at[0] if which else 1 - at[0]) * per + j),
        )
    tile = min(TILE, shape[2])
    return pl.BlockSpec((1, shape[1] // 2, tile), lambda j, at: (e, at[0] if which else 1 - at[0], j))


def whole_spec(x):
    return pl.BlockSpec(x.shape, lambda j, at: (0,) * len(x.shape))


def tiles_spec(rows, tile):
    return pl.BlockSpec((rows, tile), lambda j, at: (0, j))


def cost(rows, depth, columns):
    return pl.CostEstimate(
        flops=2 * rows * depth * columns,
        bytes_accessed=2 * (rows * depth + depth * columns + rows * columns),
        transcendentals=0,
    )


def compiler_params(**more):
    return pltpu.CompilerParams(vmem_limit_bytes=VMEM_BYTES, **more)


def partial_kernel(at, routed, gate_matrix, up_matrix, gate_out, up_out):
    gate_out[...] = dot(routed[...], gate_matrix[0]).astype(jnp.bfloat16)
    up_out[...] = dot(routed[...], up_matrix[0]).astype(jnp.bfloat16)


def partial_sums(at, routed, w_gate, w_up, e):
    rows, depth = routed.shape
    half = w_gate.shape[2] // 2
    tile = min(TILE, half)
    out = jax.ShapeDtypeStruct((rows, half), jnp.bfloat16)
    return pl.pallas_call(
        partial_kernel,
        grid_spec=pltpu.PrefetchScalarGridSpec(
            num_scalar_prefetch=1,
            grid=(half // tile,),
            in_specs=[whole_spec(routed), weight_spec(w_gate.shape, e, 2, 0), weight_spec(w_up.shape, e, 2, 0)],
            out_specs=[tiles_spec(rows, tile)] * 2,
        ),
        out_shape=[out, out],
        cost_estimate=cost(rows, depth, 2 * half),
        compiler_params=compiler_params(),
    )(at, routed, w_gate, w_up)


def hidden_kernel(at, routed, gate_matrix, up_matrix, gate_in, up_in, out):
    gate = dot(routed[...], gate_matrix[0]) + gate_in[...].astype(jnp.float32)
    up = dot(routed[...], up_matrix[0]) + up_in[...].astype(jnp.float32)
    out[...] = (gate / (1.0 + jnp.exp(-gate)) * up).astype(jnp.bfloat16)


def hidden_units(at, routed, w_gate, w_up, gate_in, up_in, e):
    rows, depth = routed.shape
    half = w_gate.shape[2] // 2
    tile = min(TILE, half)
    return pl.pallas_call(
        hidden_kernel,
        grid_spec=pltpu.PrefetchScalarGridSpec(
            num_scalar_prefetch=1,
            grid=(half // tile,),
            in_specs=[whole_spec(routed), weight_spec(w_gate.shape, e, 2, 1), weight_spec(w_up.shape, e, 2, 1)]
            + [tiles_spec(rows, tile)] * 2,
            out_specs=tiles_spec(rows, tile),
        ),
        out_shape=jax.ShapeDtypeStruct((rows, half), jnp.bfloat16),
        cost_estimate=cost(rows, depth, 2 * half),
        compiler_params=compiler_params(),
    )(at, routed, w_gate, w_up, gate_in, up_in)


def down_kernel(at, own, other, own_matrix, other_matrix, weight, out):
    summed = dot(own[...], own_matrix[0]) + dot(other[...], other_matrix[0])
    out[...] = (summed * weight[...]).astype(jnp.bfloat16)


def weighted_down(at, own, other, w_down, weight, e):
    rows, half = own.shape
    columns = w_down.shape[2]
    tile = min(TILE, columns)
    return pl.pallas_call(
        down_kernel,
        grid_spec=pltpu.PrefetchScalarGridSpec(
            num_scalar_prefetch=1,
            grid=(columns // tile,),
            in_specs=[
                whole_spec(own),
                whole_spec(other),
                weight_spec(w_down.shape, e, 1, 1),
                weight_spec(w_down.shape, e, 1, 0),
                whole_spec(weight),
            ],
            out_specs=tiles_spec(rows, tile),
        ),
        out_shape=jax.ShapeDtypeStruct((rows, columns), jnp.bfloat16),
        cost_estimate=cost(rows, 2 * half, columns),
        compiler_params=compiler_params(),
    )(at, own, other, w_down, w_down, weight)


def meet(x, z, r, n_tensor):
    barrier = pltpu.get_barrier_semaphore()
    for dz in range(n_tensor):
        for dr in range(2):
            if dz or dr:
                there = {"tensor": lax.rem(z + dz, n_tensor), "replica": lax.rem(r + dr, 2)}
                pl.semaphore_signal(barrier, inc=1, device_id=there, device_id_type=MESH)
    pl.semaphore_signal(barrier, inc=1, device_id={"expert": 1 - x}, device_id_type=MESH)
    pl.semaphore_wait(barrier, 2 * n_tensor)


def rows_at(start, size):
    return pl.ds(pl.multiple_of(start, 64), size)


def gather_kernel(n, pieces, tok, table, own_sem, own_send, own_recv, z_send, z_recv, x_send, x_recv):
    x, z, r = lax.axis_index("expert"), lax.axis_index("tensor"), lax.axis_index("replica")
    rows, width = tok.shape
    per = n // 2
    size = rows // 2 // pieces
    core_to, block_to = z // per, lax.rem(z, per)
    meet(x, z, r, n)

    def spot(block, core, start, count):
        columns = pl.ds(pl.multiple_of(block * width, width), width)
        return table.at[rows_at(core * rows + start, count), columns]

    def own_copy():
        return pltpu.make_async_copy(tok, spot(block_to, r, 0, rows), own_sem)

    def core_copy():
        return pltpu.make_async_remote_copy(
            src_ref=tok, dst_ref=spot(block_to, r, 0, rows), send_sem=own_send, recv_sem=own_recv,
            device_id={"replica": 1 - r}, device_id_type=MESH,
        )

    def z_copy(p, step):
        start = x * (rows // 2) + p * size
        return pltpu.make_async_remote_copy(
            src_ref=tok.at[rows_at(start, size)], dst_ref=spot(block_to, r, start, size),
            send_sem=z_send.at[p, step], recv_sem=z_recv.at[p, block_to, r],
            device_id={"tensor": lax.rem(z + step, n), "replica": core_to}, device_id_type=MESH,
        )

    def landed(p, block, core):
        place = spot(block, core, x * (rows // 2) + p * size, size)
        return pltpu.make_async_remote_copy(
            src_ref=place, dst_ref=place, send_sem=x_send.at[p, block, core], recv_sem=z_recv.at[p, block, core],
            device_id={"expert": 1 - x}, device_id_type=MESH,
        )

    def x_copy(p, block, core):
        place = spot(block, core, x * (rows // 2) + p * size, size)
        return pltpu.make_async_remote_copy(
            src_ref=place, dst_ref=place, send_sem=x_send.at[p, block, core], recv_sem=x_recv.at[p, block, core],
            device_id={"expert": 1 - x}, device_id_type=MESH,
        )

    for p in range(pieces):
        for step in range(1, n):
            z_copy(p, step).start()
    pl.when(core_to == r)(lambda: own_copy().start())
    pl.when(core_to != r)(lambda: core_copy().start())

    far = [(p, block, core) for p in range(pieces) for block in range(per) for core in range(2)]

    def forward(p, block, core):
        landed(p, block, core).wait_recv()
        x_copy(p, block, core).start()

    for p, block, core in far:
        pl.when(per * r + block != z)(functools.partial(forward, p, block, core))

    def finish(p, block, core):
        x_copy(p, block, core).wait()

    for p, block, core in far:
        pl.when(per * r + block != z)(functools.partial(finish, p, block, core))

    def finish_near():
        own_copy().wait()
        core_copy().wait_recv()

    pl.when(core_to == r)(finish_near)
    pl.when(core_to != r)(lambda: core_copy().wait_send())
    for p in range(pieces):
        for step in range(1, n):
            z_copy(p, step).wait_send()


def gather_tokens(tokens, n):
    rows, width = tokens.shape
    per, pieces = n // 2, 2
    dma = pltpu.SemaphoreType.DMA
    return pl.pallas_call(
        functools.partial(gather_kernel, n, pieces),
        out_shape=jax.ShapeDtypeStruct((2 * rows, per * width), tokens.dtype),
        in_specs=[pl.BlockSpec(memory_space=pl.ANY)],
        out_specs=pl.BlockSpec(memory_space=pl.ANY),
        scratch_shapes=[
            dma, dma, dma, dma((pieces, n)), dma((pieces, per, 2)), dma((pieces, per, 2)), dma((pieces, per, 2)),
        ],
        compiler_params=compiler_params(collective_id=0, has_side_effects=True),
    )(tokens)


def reduce_kernel(n, part, out, from_x, summed, from_z, final, x_send, x_recv, z_send, z_recv, f_send, f_recv):
    x, z, r = lax.axis_index("expert"), lax.axis_index("tensor"), lax.axis_index("replica")
    per = n // 2
    half, width = from_z.shape[1:]
    meet(x, z, r, n)

    def mine_of(side, block, core):
        return part.at[rows_at(core * 2 * half + side * half, half), pl.ds(block * width, width)]

    def x_copy(block, core):
        return pltpu.make_async_remote_copy(
            src_ref=mine_of(1 - x, block, core), dst_ref=from_x.at[block, core],
            send_sem=x_send.at[block, core], recv_sem=x_recv.at[block, core],
            device_id={"expert": 1 - x}, device_id_type=MESH,
        )

    def z_copy(block, core):
        return pltpu.make_async_remote_copy(
            src_ref=summed.at[block, core], dst_ref=from_z.at[z],
            send_sem=z_send.at[block, core], recv_sem=z_recv.at[z],
            device_id={"tensor": per * r + block, "replica": core}, device_id_type=MESH,
        )

    def arrival(source):
        return pltpu.make_async_remote_copy(
            src_ref=from_z.at[source], dst_ref=from_z.at[source],
            send_sem=z_send.at[0, 0], recv_sem=z_recv.at[source],
            device_id={"expert": 1 - x}, device_id_type=MESH,
        )

    def f_copy():
        return pltpu.make_async_remote_copy(
            src_ref=final.at[x], dst_ref=final.at[x], send_sem=f_send, recv_sem=f_recv,
            device_id={"expert": 1 - x}, device_id_type=MESH,
        )

    places = [(block, core) for block in range(per) for core in range(2)]

    def is_self(block, core):
        return (per * r + block == z) & (r == core)

    for block, core in places:
        x_copy(block, core).start()
    for block, core in places:
        x_copy(block, core).wait()
        total = mine_of(x, block, core)[...].astype(jnp.float32) + from_x[block, core].astype(jnp.float32)
        total = total.astype(jnp.bfloat16)
        summed[block, core] = total

        def keep(block=block, core=core):
            from_z[z] = summed[block, core]

        def send(block=block, core=core):
            z_copy(block, core).start()

        pl.when(is_self(block, core))(keep)
        pl.when(jnp.logical_not(is_self(block, core)))(send)
    for source in range(n):
        pl.when(jnp.logical_not((z == source) & (z // per == r)))(lambda source=source: arrival(source).wait_recv())
    total = from_z[0].astype(jnp.float32)
    for source in range(1, n):
        total = total + from_z[source].astype(jnp.float32)
    final[x] = total.astype(jnp.bfloat16)
    f_copy().start()
    for block, core in places:
        pl.when(jnp.logical_not(is_self(block, core)))(
            lambda block=block, core=core: z_copy(block, core).wait_send()
        )
    f_copy().wait()
    for side in range(2):
        out[pl.ds(side * half, half), :] = final[side]


def reduce_parts(part, n):
    rows, columns = part.shape
    per = n // 2
    half, width = rows // 4, columns // per
    dma, kind = pltpu.SemaphoreType.DMA, part.dtype
    return pl.pallas_call(
        functools.partial(reduce_kernel, n),
        out_shape=jax.ShapeDtypeStruct((rows // 2, width), kind),
        in_specs=[pl.BlockSpec(memory_space=pltpu.VMEM)],
        out_specs=pl.BlockSpec(memory_space=pltpu.VMEM),
        scratch_shapes=[
            pltpu.VMEM((per, 2, half, width), kind),
            pltpu.VMEM((per, 2, half, width), kind),
            pltpu.VMEM((n, half, width), kind),
            pltpu.VMEM((2, half, width), kind),
            dma((per, 2)), dma((per, 2)), dma((per, 2)), dma((n,)), dma, dma,
        ],
        compiler_params=compiler_params(collective_id=1, has_side_effects=True),
    )(part)


def body(tokens, w_gate, w_up, w_down, block_rows, block_gates, block_count):
    core = lax.axis_index("replica")
    token_rows = tokens.shape[0]
    experts = w_gate.shape[0]
    n_tensor = lax.axis_size("tensor")
    direct = lax.axis_size("expert") == 2 and n_tensor == 4
    ids, weight = slot_lists(block_rows, block_gates, block_count, core, token_rows)
    if direct:
        table = gather_tokens(tokens, n_tensor)
    else:
        full_rows = lax.all_gather(tokens, "tensor", axis=1, tiled=True)
        kept_rows = half_of(full_rows, 1, core)
        from_other = swap_cores(half_of(full_rows, 1, 1 - core))
        table = jnp.concatenate(
            [jnp.where(core == 0, kept_rows, from_other), jnp.where(core == 0, from_other, kept_rows)], axis=0
        )
    token_at = jnp.arange(2 * token_rows, dtype=jnp.int32)
    at = jnp.reshape(core, (1,)).astype(jnp.int32)

    routed, sums = [], []
    for e in range(experts):
        onehot = (ids[e][:, None] == token_at[None, :]).astype(jnp.bfloat16)
        routed.append(dot(onehot, table).astype(jnp.bfloat16))
        sums.append([swap_cores(p) for p in partial_sums(at, routed[e], w_gate, w_up, e)])
    hidden, hidden_other = [], []
    for e in range(experts):
        hidden.append(hidden_units(at, routed[e], w_gate, w_up, sums[e][0], sums[e][1], e))
        hidden_other.append(swap_cores(hidden[e]))
    parts = [
        weighted_down(at, hidden[e], hidden_other[e], w_down, weight[e][:, None], e) for e in range(experts)
    ]
    parts = jnp.concatenate(parts, axis=0)
    spread = (token_at[:, None] == ids.reshape(-1)[None, :]).astype(jnp.bfloat16)
    if direct:
        return reduce_parts(dot(spread, parts).astype(jnp.bfloat16), n_tensor)
    both = dot(spread, parts).astype(jnp.bfloat16)
    mine = half_of(both, 0, core)
    theirs = swap_cores(half_of(both, 0, 1 - core))
    low = jnp.where(core == 0, mine, theirs)
    high = jnp.where(core == 0, theirs, mine)
    own = lax.psum_scatter(jnp.concatenate([low, high], axis=1), "tensor", scatter_dimension=1, tiled=True)
    return lax.psum(own, "expert")


def solution(mesh):
    placed = (
        P(("groups", "replica"), "tensor"),
        P("expert", "replica", "tensor"),
        P("expert", "replica", "tensor"),
        P("expert", "tensor", "replica"),
        P("expert", ("groups", "replica"), None),
        P("expert", ("groups", "replica"), None),
        P("expert", ("groups", "replica")),
    )
    return jax.shard_map(
        body,
        mesh=mesh,
        in_specs=placed,
        out_specs=P(("groups", "replica"), "tensor"),
        check_vma=False,
    )
```

profile of v0, /device:TPU:25, one launch (start us, length us, event | category | flops | bytes accessed | tf_op | source)
XLA Modules:
  0.0 213.9 jit_solution(905189484952457437)
XLA Ops:
  0.0 0.7 convert_bitcast_fusion
  0.7 0.7 convert_element_type.54
  1.4 0.7 pad_maximum_fusion
  2.1 0.7 collective-permute-start
  2.9 1.1 copy-done.1
  4.0 27.0 %shard_map.73 = bf16[1024,1536]{1,0:T(8,128)(2,1)S(1)} custom-call(bf16[512,768]{1,0:T(8,128)(2,1)S(1)} %copy-done.1), custom_call_target="tpu_custom_call" | custom-call | tf_op jit(solution)/shard_map/pallas_call | solution.py:260
  31.6 3.0 %convolution_convert_fusion.routed = bf16[768,1536]{1,0:T(8,128)(2,1)S(1)} fusion(bf16[1024,1536]{1,0:T(8,128)(2,1)S(1)} %shard_map.73, s32[768]{0:T(1024)S(1)} %get-tuple-element.24), kind=kOutput, calls=%fused_computation.6 | convolution fusion | flops 2417885184 | bytes 5508096 | tf_op jit(solution)/shard_map/dot_general | solution.py:28
  34.6 3.0 %convolution_convert_fusion.1.routed = bf16[768,1536]{1,0:T(8,128)(2,1)S(1)} fusion(bf16[1024,1536]{1,0:T(8,128)(2,1)S(1)} %shard_map.73, s32[768]{0:T(1024)S(1)} %get-tuple-element.23), kind=kOutput, calls=%fused_computation.7 | convolution fusion | flops 2417885184 | bytes 5508096 | tf_op jit(solution)/shard_map/dot_general | solution.py:28
  37.6 13.5 %shard_map.74 = (bf16[768,2048]{1,0:T(8,128)(2,1)S(1)}, bf16[768,2048]{1,0:T(8,128)(2,1)}) custom-call(s32[1]{0:T(128)} %bitcast.3.at, bf16[768,1536]{1,0:T(8,128)(2,1)S(1)} %convolution_convert_fusion.1.routed, bf16[2,1536,4096]{2,1,0:T(8,128)(2,1)} %gate_matrix.7, bf16[2,1536,4096]{2,1,0:T(8,128)(2,1)} %up_matrix.7), custom_call_target="tpu_custom_call" | custom-call | flops 9663676416 | bytes 21233664 | tf_op jit(solution)/shard_map/pallas_call | solution.py:98
  51.1 18.2 %collective-permute-start.1 = (bf16[768,2048]{1,0:T(8,128)(2,1)S(1)}, bf16[768,2048]{1,0:T(8,128)(2,1)S(1)}, u32[]{:S(2)}, u32[]{:S(2)}) collective-permute-start(bf16[768,2048]{1,0:T(8,128)(2,1)S(1)} %get-tuple-element.9), channel_id=1, source_target_pairs={{0,1},{1,0},{2,3},{3,2},{4,5},{5,4},{6,7},{7,6},{8,9},{9,8},{10,11... | collective-permute-start | bytes 9437192 | tf_op jit(solution)/shard_map/ppermute | solution.py:19
  69.4 13.5 %shard_map.77 = (bf16[768,2048]{1,0:T(8,128)(2,1)S(1)}, bf16[768,2048]{1,0:T(8,128)(2,1)}) custom-call(s32[1]{0:T(128)} %bitcast.3.at, bf16[768,1536]{1,0:T(8,128)(2,1)S(1)} %convolution_convert_fusion.routed, bf16[2,1536,4096]{2,1,0:T(8,128)(2,1)} %gate_matrix.7, bf16[2,1536,4096]{2,1,0:T(8,128)(2,1)} %up_matrix.7), custom_call_target="tpu_custom_call" | custom-call | flops 9663676416 | bytes 21233664 | tf_op jit(solution)/shard_map/pallas_call | solution.py:98
  82.8 0.5 collective-permute-start.4
  83.4 1.7 copy-done.2
  85.0 13.3 %shard_map.75.own = bf16[768,2048]{1,0:T(8,128)(2,1)S(1)} custom-call(s32[1]{0:T(128)} %bitcast.3.at, bf16[768,1536]{1,0:T(8,128)(2,1)S(1)} %convolution_convert_fusion.1.routed, bf16[2,1536,4096]{2,1,0:T(8,128)(2,1)} %gate_matrix.7, bf16[2,1536,4096]{2,1,0:T(8,128)(2,1)} %up_matrix.7, bf16[768,2048]{1,0:T(8,128)(2,1)} %copy-done.2, ...), custom_call_target="tpu_custom_call" | custom-call | flops 9663676416 | bytes 21233664 | tf_op jit(solution)/shard_map/pallas_call | solution.py:122
  98.4 0.6 collective-permute-start.3
  98.9 14.0 %shard_map.78.own = bf16[768,2048]{1,0:T(8,128)(2,1)} custom-call(s32[1]{0:T(128)} %bitcast.3.at, bf16[768,1536]{1,0:T(8,128)(2,1)S(1)} %convolution_convert_fusion.routed, bf16[2,1536,4096]{2,1,0:T(8,128)(2,1)} %gate_matrix.7, bf16[2,1536,4096]{2,1,0:T(8,128)(2,1)} %up_matrix.7, bf16[768,2048]{1,0:T(8,128)(2,1)} %collective-permute-done.4.gate_in, ...), custom_call_target="tpu_custom_call" | custom-call | flops 9663676416 | bytes 21233664 | tf_op jit(solution)/shard_map/pallas_call | solution.py:122
  113.0 0.2 copy.15
  113.2 0.9 copy.13
  114.2 1.0 copy-done
  115.2 13.6 %shard_map.76 = bf16[768,1536]{1,0:T(8,128)(2,1)S(1)} custom-call(s32[1]{0:T(128)} %bitcast.3.at, bf16[768,2048]{1,0:T(8,128)(2,1)S(1)} %shard_map.75.own, bf16[768,2048]{1,0:T(8,128)(2,1)} %collective-permute-done.3.other, bf16[2,4096,1536]{2,1,0:T(8,128)(2,1)} %other_matrix.3, bf16[2,4096,1536]{2,1,0:T(8,128)(2,1)} %other_matrix.3, f32[768,1]{1,0:T(8,128)S(1)} %bitcast.26), custom_call_target="tpu_custom_call" | custom-call | flops 9663676416 | bytes 21233664 | tf_op jit(solution)/shard_map/pallas_call | solution.py:146
  128.8 14.7 %shard_map.79 = bf16[768,1536]{1,0:T(8,128)(2,1)S(1)} custom-call(s32[1]{0:T(128)} %bitcast.3.at, bf16[768,2048]{1,0:T(8,128)(2,1)} %shard_map.78.own, bf16[768,2048]{1,0:T(8,128)(2,1)} %collective-permute-done.6.other, bf16[2,4096,1536]{2,1,0:T(8,128)(2,1)} %other_matrix.3, bf16[2,4096,1536]{2,1,0:T(8,128)(2,1)} %other_matrix.3, f32[768,1]{1,0:T(8,128)S(1)} %bitcast.25), custom_call_target="tpu_custom_call" | custom-call | flops 9663676416 | bytes 21233664 | tf_op jit(solution)/shard_map/pallas_call | solution.py:146
  143.6 5.3 %fusion.4.part = bf16[1024,1536]{1,0:T(8,128)(2,1)S(1)} fusion(bf16[768,1536]{1,0:T(8,128)(2,1)S(1)} %shard_map.79, bf16[768,1536]{1,0:T(8,128)(2,1)S(1)} %shard_map.76, s32[1536]{0:T(1024)S(1)} %convert_element_type.61), kind=kOutput, calls=%fused_computation.5 | convolution fusion | flops 4844421120 | bytes 7870464 | tf_op jit(solution)/shard_map/dot_general | solution.py:28
  148.9 64.0 %shard_map.80 = bf16[512,768]{1,0:T(8,128)(2,1)S(1)} custom-call(bf16[1024,1536]{1,0:T(8,128)(2,1)S(1)} %fusion.4.part), custom_call_target="tpu_custom_call" | custom-call | tf_op jit(solution)/shard_map/pallas_call | solution.py:350
  213.0 0.9 copy.21
  (32 shorter events, 0.6 us)
Async XLA Ops:
  0.0 31.1 %copy-start.3 = (f32[2,1,512]{2,1,0:T(1,128)S(1)}, f32[2,1,512]{2,1,0:T(1,128)}, u32[]{:S(2)}) copy-start(f32[2,1,512]{2,1,0:T(1,128)} %param.12) | copy-start | bytes 12292
  2.1 28.9 %collective-permute-start = (f32[2,3,512]{2,1,0:T(4,128)S(1)}, f32[2,3,512]{2,1,0:T(4,128)S(1)}, u32[]{:S(2)}, u32[]{:S(2)}) collective-permute-start(f32[2,3,512]{2,1,0:T(4,128)S(1)} %pad_maximum_fusion), channel_id=1, source_target_pairs={{0,1},{1,0},{2,3},{3,2},{4,5},{5,4},{6,7},{7,6},{8,9},{9,8},{10,11... | collective-permute-start | bytes 36872 | tf_op jit(solution)/shard_map/ppermute | solution.py:19
  2.9 1.1 copy-start.1
  51.1 32.2 %collective-permute-start.1 = (bf16[768,2048]{1,0:T(8,128)(2,1)S(1)}, bf16[768,2048]{1,0:T(8,128)(2,1)S(1)}, u32[]{:S(2)}, u32[]{:S(2)}) collective-permute-start(bf16[768,2048]{1,0:T(8,128)(2,1)S(1)} %get-tuple-element.9), channel_id=1, source_target_pairs={{0,1},{1,0},{2,3},{3,2},{4,5},{5,4},{6,7},{7,6},{8,9},{9,8},{10,11... | collective-permute-start | bytes 9437192 | tf_op jit(solution)/shard_map/ppermute | solution.py:19
  69.3 15.7 %collective-permute-start.2 = (bf16[768,2048]{1,0:T(8,128)(2,1)}, bf16[768,2048]{1,0:T(8,128)(2,1)}, u32[]{:S(2)}, u32[]{:S(2)}) collective-permute-start(bf16[768,2048]{1,0:T(8,128)(2,1)} %get-tuple-element.10), channel_id=1, source_target_pairs={{0,1},{1,0},{2,3},{3,2},{4,5},{5,4},{6,7},{7,6},{8,9},{9,8},{10,11... | collective-permute-start | bytes 9437192 | tf_op jit(solution)/shard_map/ppermute | solution.py:19
  82.8 16.1 %collective-permute-start.4 = (bf16[768,2048]{1,0:T(8,128)(2,1)S(1)}, bf16[768,2048]{1,0:T(8,128)(2,1)}, u32[]{:S(2)}, u32[]{:S(2)}) collective-permute-start(bf16[768,2048]{1,0:T(8,128)(2,1)S(1)} %get-tuple-element.11), channel_id=1, source_target_pairs={{0,1},{1,0},{2,3},{3,2},{4,5},{5,4},{6,7},{7,6},{8,9},{9,8},{10,11... | collective-permute-start | bytes 9437192 | tf_op jit(solution)/shard_map/ppermute | solution.py:19
  83.4 15.6 %collective-permute-start.5 = (bf16[768,2048]{1,0:T(8,128)(2,1)}, bf16[768,2048]{1,0:T(8,128)(2,1)}, u32[]{:S(2)}, u32[]{:S(2)}) collective-permute-start(bf16[768,2048]{1,0:T(8,128)(2,1)} %get-tuple-element.12), channel_id=1, source_target_pairs={{0,1},{1,0},{2,3},{3,2},{4,5},{5,4},{6,7},{7,6},{8,9},{9,8},{10,11... | collective-permute-start | bytes 9437192 | tf_op jit(solution)/shard_map/ppermute | solution.py:19
  83.4 1.7 copy-start.2
  98.4 15.8 %collective-permute-start.3 = (bf16[768,2048]{1,0:T(8,128)(2,1)S(1)}, bf16[768,2048]{1,0:T(8,128)(2,1)}, u32[]{:S(2)}, u32[]{:S(2)}) collective-permute-start(bf16[768,2048]{1,0:T(8,128)(2,1)S(1)} %shard_map.75.own), channel_id=1, source_target_pairs={{0,1},{1,0},{2,3},{3,2},{4,5},{5,4},{6,7},{7,6},{8,9},{9,8},{10,11... | collective-permute-start | bytes 9437192 | tf_op jit(solution)/shard_map/ppermute | solution.py:19
  113.0 15.8 %collective-permute-start.6 = (bf16[768,2048]{1,0:T(8,128)(2,1)}, bf16[768,2048]{1,0:T(8,128)(2,1)}, u32[]{:S(2)}, u32[]{:S(2)}) collective-permute-start(bf16[768,2048]{1,0:T(8,128)(2,1)} %shard_map.78.own), channel_id=1, source_target_pairs={{0,1},{1,0},{2,3},{3,2},{4,5},{5,4},{6,7},{7,6},{8,9},{9,8},{10,11... | collective-permute-start | bytes 9437192 | tf_op jit(solution)/shard_map/ppermute | solution.py:19
  114.2 1.0 copy-start
where the time goes:
time: 214 us
  Pallas kernels  174 us (81%)
  starting transfers between devices  20.1 us (9%)
  matrix products  11.3 us (5%)
  local copies, waits for them, and re-layouts  5.89 us (3%)
  other arithmetic  2.54 us (1%)
    pallas_call x1, Pallas kernels, reduce_parts(): pl.pallas_call(functools.partial(reduce_kernel, n), out_shape=jax.ShapeDt...  64 us
    pallas_call x2, Pallas kernels, weighted_down(): pl.pallas_call(down_kernel, grid_spec=pltpu.PrefetchScalarGridSpec(num_sc...  28.4 us
    pallas_call x2, Pallas kernels, hidden_units(): pl.pallas_call(hidden_kernel, grid_spec=pltpu.PrefetchScalarGridSpec(num_...  27.4 us
    pallas_call x1, Pallas kernels, gather_tokens(): pl.pallas_call(functools.partial(gather_kernel, n, pieces), out_shape=jax...  27 us
    pallas_call x2, Pallas kernels, partial_sums(): pl.pallas_call(partial_kernel, grid_spec=pltpu.PrefetchScalarGridSpec(num...  27 us
    ppermute x7, starting transfers between devices, swap_cores(): return lax.ppermute(x, 'replica', SWAP)  20.1 us
    dot_general x3, matrix products, dot(): return jnp.dot(a, b, preferred_element_type=jnp.float32)  11.3 us
    unnamed x14, local copies, waits for them, and re-layouts  5.81 us
  transfers between devices with their start and end apart: 7, of which 0 were waited for; matrix products, arithmetic and copies ran while one was open for 1% of the time, Pallas kernels for 38%

commit v1 on v0

--- a/solution.py
+++ b/solution.py
@@ -178,7 +178,7 @@
     return pl.ds(pl.multiple_of(start, 64), size)
 
 
-def gather_kernel(n, pieces, tok, table, own_sem, own_send, own_recv, z_send, z_recv, x_send, x_recv):
+def gather_kernel(n, pieces, tok, table, own_sem, own_send, own_recv, z_send, z_recv, relay_send, x_send, x_recv):
     x, z, r = lax.axis_index("expert"), lax.axis_index("tensor"), lax.axis_index("replica")
     rows, width = tok.shape
     per = n // 2
@@ -199,12 +199,20 @@
             device_id={"replica": 1 - r}, device_id_type=MESH,
         )
 
-    def z_copy(p, step):
+    def z_copy(p, way):
         start = x * (rows // 2) + p * size
         return pltpu.make_async_remote_copy(
             src_ref=tok.at[rows_at(start, size)], dst_ref=spot(block_to, r, start, size),
-            send_sem=z_send.at[p, step], recv_sem=z_recv.at[p, block_to, r],
-            device_id={"tensor": lax.rem(z + step, n), "replica": core_to}, device_id_type=MESH,
+            send_sem=z_send.at[p, way], recv_sem=z_recv.at[p, block_to, r],
+            device_id={"tensor": z - 1 + 2 * way, "replica": core_to}, device_id_type=MESH,
+        )
+
+    def relay_copy(p, block, core, way):
+        place = spot(block, core, x * (rows // 2) + p * size, size)
+        return pltpu.make_async_remote_copy(
+            src_ref=place, dst_ref=place,
+            send_sem=relay_send.at[p, block, core], recv_sem=z_recv.at[p, block, core],
+            device_id={"tensor": z - 1 + 2 * way}, device_id_type=MESH,
         )
 
     def landed(p, block, core):
@@ -221,16 +229,24 @@
             device_id={"expert": 1 - x}, device_id_type=MESH,
         )
 
+    onward = ((z > 0), (z < n - 1))
     for p in range(pieces):
-        for step in range(1, n):
-            z_copy(p, step).start()
+        for way in range(2):
+            pl.when(onward[way])(lambda p=p, way=way: z_copy(p, way).start())
     pl.when(core_to == r)(lambda: own_copy().start())
     pl.when(core_to != r)(lambda: core_copy().start())
 
-    far = [(p, block, core) for p in range(pieces) for block in range(per) for core in range(2)]
+    above = z // (per * (r + 1))
+    far = [(p, k + above * (per - 1 - 2 * k), core) for k in range(per) for p in range(pieces) for core in range(2)]
+
+    def passes(block, way):
+        source = per * r + block
+        return onward[way] & ((source < z) if way else (source > z))
 
     def forward(p, block, core):
         landed(p, block, core).wait_recv()
+        for way in range(2):
+            pl.when(passes(block, way))(lambda way=way: relay_copy(p, block, core, way).start())
         x_copy(p, block, core).start()
 
     for p, block, core in far:
@@ -238,6 +254,8 @@
 
     def finish(p, block, core):
         x_copy(p, block, core).wait()
+        for way in range(2):
+            pl.when(passes(block, way))(lambda way=way: relay_copy(p, block, core, way).wait_send())
 
     for p, block, core in far:
         pl.when(per * r + block != z)(functools.partial(finish, p, block, core))
@@ -249,13 +267,13 @@
     pl.when(core_to == r)(finish_near)
     pl.when(core_to != r)(lambda: core_copy().wait_send())
     for p in range(pieces):
-        for step in range(1, n):
-            z_copy(p, step).wait_send()
+        for way in range(2):
+            pl.when(onward[way])(lambda p=p, way=way: z_copy(p, way).wait_send())
 
 
 def gather_tokens(tokens, n):
     rows, width = tokens.shape
-    per, pieces = n // 2, 2
+    per, pieces = n // 2, 4
     dma = pltpu.SemaphoreType.DMA
     return pl.pallas_call(
         functools.partial(gather_kernel, n, pieces),
@@ -263,7 +281,7 @@
         in_specs=[pl.BlockSpec(memory_space=pl.ANY)],
         out_specs=pl.BlockSpec(memory_space=pl.ANY),
         scratch_shapes=[
-            dma, dma, dma, dma((pieces, n)), dma((pieces, per, 2)), dma((pieces, per, 2)), dma((pieces, per, 2)),
+            dma, dma, dma, dma((pieces, 2)), *[dma((pieces, per, 2))] * 4,
         ],
         compiler_params=compiler_params(collective_id=0, has_side_effects=True),
     )(tokens)

time: 214 us -> 202 us (0.944)
  Pallas kernels: 174 us -> 163 us
    pallas_call x1, Pallas kernels: 27 us -> 17.3 us  [gather_tokens(): pl.pallas_call(functools.partial(gather_kernel, n, pieces), out_shape=jax...]
  transfers between devices with their start and end apart: 7 -> 7, of which waited for: 0 -> 0; matrix products, arithmetic and copies ran while one was open for 1% -> 1% of each run, Pallas kernels for 38% -> 36%
where the time goes in v1:
time: 202 us
  Pallas kernels  163 us (81%)
  starting transfers between devices  18.4 us (9%)
  matrix products  11.3 us (6%)
  local copies, waits for them, and re-layouts  5.89 us (3%)
  other arithmetic  2.54 us (1%)
    pallas_call x1, Pallas kernels, reduce_parts(): pl.pallas_call(functools.partial(reduce_kernel, n), out_shape=jax.ShapeDt...  63.3 us
    pallas_call x2, Pallas kernels, weighted_down(): pl.pallas_call(down_kernel, grid_spec=pltpu.PrefetchScalarGridSpec(num_sc...  28.4 us
    pallas_call x2, Pallas kernels, hidden_units(): pl.pallas_call(hidden_kernel, grid_spec=pltpu.PrefetchScalarGridSpec(num_...  27.4 us
    pallas_call x2, Pallas kernels, partial_sums(): pl.pallas_call(partial_kernel, grid_spec=pltpu.PrefetchScalarGridSpec(num...  27 us
    ppermute x7, starting transfers between devices, swap_cores(): return lax.ppermute(x, 'replica', SWAP)  18.4 us
    pallas_call x1, Pallas kernels, gather_tokens(): pl.pallas_call(functools.partial(gather_kernel, n, pieces), out_shape=jax...  17.3 us
    dot_general x3, matrix products, dot(): return jnp.dot(a, b, preferred_element_type=jnp.float32)  11.3 us
    unnamed x14, local copies, waits for them, and re-layouts  5.81 us
  transfers between devices with their start and end apart: 7, of which 0 were waited for; matrix products, arithmetic and copies ran while one was open for 1% of the time, Pallas kernels for 36%

profile of v1, /device:TPU:25, one launch (start us, length us, event | category | flops | bytes accessed | tf_op | source)
XLA Modules:
  0.0 201.7 jit_solution(5094591632730485671)
XLA Ops:
  0.0 0.7 convert_bitcast_fusion
  0.7 0.7 convert_element_type.54
  1.4 0.7 pad_maximum_fusion
  2.1 0.7 collective-permute-start
  2.9 1.1 copy-done.1
  4.0 17.3 %shard_map.73 = bf16[1024,1536]{1,0:T(8,128)(2,1)S(1)} custom-call(bf16[512,768]{1,0:T(8,128)(2,1)S(1)} %copy-done.1), custom_call_target="tpu_custom_call" | custom-call | tf_op jit(solution)/shard_map/pallas_call | solution.py:278
  21.9 3.0 %convolution_convert_fusion.routed = bf16[768,1536]{1,0:T(8,128)(2,1)S(1)} fusion(bf16[1024,1536]{1,0:T(8,128)(2,1)S(1)} %shard_map.73, s32[768]{0:T(1024)S(1)} %get-tuple-element.24), kind=kOutput, calls=%fused_computation.6 | convolution fusion | flops 2417885184 | bytes 5508096 | tf_op jit(solution)/shard_map/dot_general | solution.py:28
  24.9 3.0 %convolution_convert_fusion.1.routed = bf16[768,1536]{1,0:T(8,128)(2,1)S(1)} fusion(bf16[1024,1536]{1,0:T(8,128)(2,1)S(1)} %shard_map.73, s32[768]{0:T(1024)S(1)} %get-tuple-element.23), kind=kOutput, calls=%fused_computation.7 | convolution fusion | flops 2417885184 | bytes 5508096 | tf_op jit(solution)/shard_map/dot_general | solution.py:28
  27.9 13.5 %shard_map.74 = (bf16[768,2048]{1,0:T(8,128)(2,1)S(1)}, bf16[768,2048]{1,0:T(8,128)(2,1)}) custom-call(s32[1]{0:T(128)} %bitcast.3.at, bf16[768,1536]{1,0:T(8,128)(2,1)S(1)} %convolution_convert_fusion.1.routed, bf16[2,1536,4096]{2,1,0:T(8,128)(2,1)} %gate_matrix.7, bf16[2,1536,4096]{2,1,0:T(8,128)(2,1)} %up_matrix.7), custom_call_target="tpu_custom_call" | custom-call | flops 9663676416 | bytes 21233664 | tf_op jit(solution)/shard_map/pallas_call | solution.py:98
  41.4 16.6 %collective-permute-start.1 = (bf16[768,2048]{1,0:T(8,128)(2,1)S(1)}, bf16[768,2048]{1,0:T(8,128)(2,1)S(1)}, u32[]{:S(2)}, u32[]{:S(2)}) collective-permute-start(bf16[768,2048]{1,0:T(8,128)(2,1)S(1)} %get-tuple-element.9), channel_id=1, source_target_pairs={{0,1},{1,0},{2,3},{3,2},{4,5},{5,4},{6,7},{7,6},{8,9},{9,8},{10,11... | collective-permute-start | bytes 9437192 | tf_op jit(solution)/shard_map/ppermute | solution.py:19
  58.0 13.5 %shard_map.77 = (bf16[768,2048]{1,0:T(8,128)(2,1)S(1)}, bf16[768,2048]{1,0:T(8,128)(2,1)}) custom-call(s32[1]{0:T(128)} %bitcast.3.at, bf16[768,1536]{1,0:T(8,128)(2,1)S(1)} %convolution_convert_fusion.routed, bf16[2,1536,4096]{2,1,0:T(8,128)(2,1)} %gate_matrix.7, bf16[2,1536,4096]{2,1,0:T(8,128)(2,1)} %up_matrix.7), custom_call_target="tpu_custom_call" | custom-call | flops 9663676416 | bytes 21233664 | tf_op jit(solution)/shard_map/pallas_call | solution.py:98
  71.4 0.5 collective-permute-start.4
  72.0 1.7 copy-done.2
  73.6 13.3 %shard_map.75.own = bf16[768,2048]{1,0:T(8,128)(2,1)S(1)} custom-call(s32[1]{0:T(128)} %bitcast.3.at, bf16[768,1536]{1,0:T(8,128)(2,1)S(1)} %convolution_convert_fusion.1.routed, bf16[2,1536,4096]{2,1,0:T(8,128)(2,1)} %gate_matrix.7, bf16[2,1536,4096]{2,1,0:T(8,128)(2,1)} %up_matrix.7, bf16[768,2048]{1,0:T(8,128)(2,1)} %copy-done.2, ...), custom_call_target="tpu_custom_call" | custom-call | flops 9663676416 | bytes 21233664 | tf_op jit(solution)/shard_map/pallas_call | solution.py:122
  87.0 0.6 collective-permute-start.3
  87.5 14.0 %shard_map.78.own = bf16[768,2048]{1,0:T(8,128)(2,1)} custom-call(s32[1]{0:T(128)} %bitcast.3.at, bf16[768,1536]{1,0:T(8,128)(2,1)S(1)} %convolution_convert_fusion.routed, bf16[2,1536,4096]{2,1,0:T(8,128)(2,1)} %gate_matrix.7, bf16[2,1536,4096]{2,1,0:T(8,128)(2,1)} %up_matrix.7, bf16[768,2048]{1,0:T(8,128)(2,1)} %collective-permute-done.4.gate_in, ...), custom_call_target="tpu_custom_call" | custom-call | flops 9663676416 | bytes 21233664 | tf_op jit(solution)/shard_map/pallas_call | solution.py:122
  101.6 0.2 copy.15
  101.8 0.9 copy.13
  102.8 1.0 copy-done
  103.8 13.6 %shard_map.76 = bf16[768,1536]{1,0:T(8,128)(2,1)S(1)} custom-call(s32[1]{0:T(128)} %bitcast.3.at, bf16[768,2048]{1,0:T(8,128)(2,1)S(1)} %shard_map.75.own, bf16[768,2048]{1,0:T(8,128)(2,1)} %collective-permute-done.3.other, bf16[2,4096,1536]{2,1,0:T(8,128)(2,1)} %other_matrix.3, bf16[2,4096,1536]{2,1,0:T(8,128)(2,1)} %other_matrix.3, f32[768,1]{1,0:T(8,128)S(1)} %bitcast.26), custom_call_target="tpu_custom_call" | custom-call | flops 9663676416 | bytes 21233664 | tf_op jit(solution)/shard_map/pallas_call | solution.py:146
  117.4 14.7 %shard_map.79 = bf16[768,1536]{1,0:T(8,128)(2,1)S(1)} custom-call(s32[1]{0:T(128)} %bitcast.3.at, bf16[768,2048]{1,0:T(8,128)(2,1)} %shard_map.78.own, bf16[768,2048]{1,0:T(8,128)(2,1)} %collective-permute-done.6.other, bf16[2,4096,1536]{2,1,0:T(8,128)(2,1)} %other_matrix.3, bf16[2,4096,1536]{2,1,0:T(8,128)(2,1)} %other_matrix.3, f32[768,1]{1,0:T(8,128)S(1)} %bitcast.25), custom_call_target="tpu_custom_call" | custom-call | flops 9663676416 | bytes 21233664 | tf_op jit(solution)/shard_map/pallas_call | solution.py:146
  132.2 5.3 %fusion.4.part = bf16[1024,1536]{1,0:T(8,128)(2,1)S(1)} fusion(bf16[768,1536]{1,0:T(8,128)(2,1)S(1)} %shard_map.79, bf16[768,1536]{1,0:T(8,128)(2,1)S(1)} %shard_map.76, s32[1536]{0:T(1024)S(1)} %convert_element_type.61), kind=kOutput, calls=%fused_computation.5 | convolution fusion | flops 4844421120 | bytes 7870464 | tf_op jit(solution)/shard_map/dot_general | solution.py:28
  137.5 63.3 %shard_map.80 = bf16[512,768]{1,0:T(8,128)(2,1)S(1)} custom-call(bf16[1024,1536]{1,0:T(8,128)(2,1)S(1)} %fusion.4.part), custom_call_target="tpu_custom_call" | custom-call | tf_op jit(solution)/shard_map/pallas_call | solution.py:368
  200.8 0.9 copy.21
  (32 shorter events, 0.6 us)
Async XLA Ops:
  0.0 21.3 %copy-start.3 = (f32[2,1,512]{2,1,0:T(1,128)S(1)}, f32[2,1,512]{2,1,0:T(1,128)}, u32[]{:S(2)}) copy-start(f32[2,1,512]{2,1,0:T(1,128)} %param.12) | copy-start | bytes 12292
  2.1 19.2 %collective-permute-start = (f32[2,3,512]{2,1,0:T(4,128)S(1)}, f32[2,3,512]{2,1,0:T(4,128)S(1)}, u32[]{:S(2)}, u32[]{:S(2)}) collective-permute-start(f32[2,3,512]{2,1,0:T(4,128)S(1)} %pad_maximum_fusion), channel_id=1, source_target_pairs={{0,1},{1,0},{2,3},{3,2},{4,5},{5,4},{6,7},{7,6},{8,9},{9,8},{10,11... | collective-permute-start | bytes 36872 | tf_op jit(solution)/shard_map/ppermute | solution.py:19
  2.9 1.1 copy-start.1
  41.4 30.6 %collective-permute-start.1 = (bf16[768,2048]{1,0:T(8,128)(2,1)S(1)}, bf16[768,2048]{1,0:T(8,128)(2,1)S(1)}, u32[]{:S(2)}, u32[]{:S(2)}) collective-permute-start(bf16[768,2048]{1,0:T(8,128)(2,1)S(1)} %get-tuple-element.9), channel_id=1, source_target_pairs={{0,1},{1,0},{2,3},{3,2},{4,5},{5,4},{6,7},{7,6},{8,9},{9,8},{10,11... | collective-permute-start | bytes 9437192 | tf_op jit(solution)/shard_map/ppermute | solution.py:19
  58.0 15.7 %collective-permute-start.2 = (bf16[768,2048]{1,0:T(8,128)(2,1)}, bf16[768,2048]{1,0:T(8,128)(2,1)}, u32[]{:S(2)}, u32[]{:S(2)}) collective-permute-start(bf16[768,2048]{1,0:T(8,128)(2,1)} %get-tuple-element.10), channel_id=1, source_target_pairs={{0,1},{1,0},{2,3},{3,2},{4,5},{5,4},{6,7},{7,6},{8,9},{9,8},{10,11... | collective-permute-start | bytes 9437192 | tf_op jit(solution)/shard_map/ppermute | solution.py:19
  71.4 16.1 %collective-permute-start.4 = (bf16[768,2048]{1,0:T(8,128)(2,1)S(1)}, bf16[768,2048]{1,0:T(8,128)(2,1)}, u32[]{:S(2)}, u32[]{:S(2)}) collective-permute-start(bf16[768,2048]{1,0:T(8,128)(2,1)S(1)} %get-tuple-element.11), channel_id=1, source_target_pairs={{0,1},{1,0},{2,3},{3,2},{4,5},{5,4},{6,7},{7,6},{8,9},{9,8},{10,11... | collective-permute-start | bytes 9437192 | tf_op jit(solution)/shard_map/ppermute | solution.py:19
  72.0 15.6 %collective-permute-start.5 = (bf16[768,2048]{1,0:T(8,128)(2,1)}, bf16[768,2048]{1,0:T(8,128)(2,1)}, u32[]{:S(2)}, u32[]{:S(2)}) collective-permute-start(bf16[768,2048]{1,0:T(8,128)(2,1)} %get-tuple-element.12), channel_id=1, source_target_pairs={{0,1},{1,0},{2,3},{3,2},{4,5},{5,4},{6,7},{7,6},{8,9},{9,8},{10,11... | collective-permute-start | bytes 9437192 | tf_op jit(solution)/shard_map/ppermute | solution.py:19
  72.0 1.7 copy-start.2
  87.0 15.8 %collective-permute-start.3 = (bf16[768,2048]{1,0:T(8,128)(2,1)S(1)}, bf16[768,2048]{1,0:T(8,128)(2,1)}, u32[]{:S(2)}, u32[]{:S(2)}) collective-permute-start(bf16[768,2048]{1,0:T(8,128)(2,1)S(1)} %shard_map.75.own), channel_id=1, source_target_pairs={{0,1},{1,0},{2,3},{3,2},{4,5},{5,4},{6,7},{7,6},{8,9},{9,8},{10,11... | collective-permute-start | bytes 9437192 | tf_op jit(solution)/shard_map/ppermute | solution.py:19
  101.6 15.8 %collective-permute-start.6 = (bf16[768,2048]{1,0:T(8,128)(2,1)}, bf16[768,2048]{1,0:T(8,128)(2,1)}, u32[]{:S(2)}, u32[]{:S(2)}) collective-permute-start(bf16[768,2048]{1,0:T(8,128)(2,1)} %shard_map.78.own), channel_id=1, source_target_pairs={{0,1},{1,0},{2,3},{3,2},{4,5},{5,4},{6,7},{7,6},{8,9},{9,8},{10,11... | collective-permute-start | bytes 9437192 | tf_op jit(solution)/shard_map/ppermute | solution.py:19
  102.8 1.0 copy-start

commit v2 on v1

--- a/solution.py
+++ b/solution.py
@@ -12,6 +12,7 @@
 VMEM_BYTES = 48 * 1024 * 1024
 MESH = pl.DeviceIdType.MESH
 PAIR_BLOCKS = 6
+SHORT_BLOCKS = 4
 SWAP = ((0, 1), (1, 0))
 
 
@@ -50,7 +51,7 @@
     pick = pick[:, :, :, None]
     ids = jnp.sum(jnp.where(pick, rows, 0.0), axis=2).reshape(experts, PAIR_BLOCKS * BLOCK)
     weight = jnp.sum(jnp.where(pick, gates, 0.0), axis=2).reshape(experts, PAIR_BLOCKS * BLOCK)
-    return ids.astype(jnp.int32), weight
+    return ids.astype(jnp.int32), weight, (n_first + n_second)[:, 0]
 
 
 def weight_spec(shape, e, split, which):
@@ -85,9 +86,18 @@
     return pltpu.CompilerParams(vmem_limit_bytes=VMEM_BYTES, **more)
 
 
-def partial_kernel(at, routed, gate_matrix, up_matrix, gate_out, up_out):
-    gate_out[...] = dot(routed[...], gate_matrix[0]).astype(jnp.bfloat16)
-    up_out[...] = dot(routed[...], up_matrix[0]).astype(jnp.bfloat16)
+def for_live(at, e, run):
+    short = at[1 + e] <= SHORT_BLOCKS
+    pl.when(short)(lambda: run(SHORT_BLOCKS * BLOCK))
+    pl.when(jnp.logical_not(short))(lambda: run(PAIR_BLOCKS * BLOCK))
+
+
+def partial_kernel(e, at, routed, gate_matrix, up_matrix, gate_out, up_out):
+    def run(rows):
+        gate_out[:rows] = dot(routed[:rows], gate_matrix[0]).astype(jnp.bfloat16)
+        up_out[:rows] = dot(routed[:rows], up_matrix[0]).astype(jnp.bfloat16)
+
+    for_live(at, e, run)
 
 
 def partial_sums(at, routed, w_gate, w_up, e):
@@ -96,7 +106,7 @@
     tile = min(TILE, half)
     out = jax.ShapeDtypeStruct((rows, half), jnp.bfloat16)
     return pl.pallas_call(
-        partial_kernel,
+        functools.partial(partial_kernel, e),
         grid_spec=pltpu.PrefetchScalarGridSpec(
             num_scalar_prefetch=1,
             grid=(half // tile,),
@@ -109,10 +119,13 @@
     )(at, routed, w_gate, w_up)
 
 
-def hidden_kernel(at, routed, gate_matrix, up_matrix, gate_in, up_in, out):
-    gate = dot(routed[...], gate_matrix[0]) + gate_in[...].astype(jnp.float32)
-    up = dot(routed[...], up_matrix[0]) + up_in[...].astype(jnp.float32)
-    out[...] = (gate / (1.0 + jnp.exp(-gate)) * up).astype(jnp.bfloat16)
+def hidden_kernel(e, at, routed, gate_matrix, up_matrix, gate_in, up_in, out):
+    def run(rows):
+        gate = dot(routed[:rows], gate_matrix[0]) + gate_in[:rows].astype(jnp.float32)
+        up = dot(routed[:rows], up_matrix[0]) + up_in[:rows].astype(jnp.float32)
+        out[:rows] = (gate / (1.0 + jnp.exp(-gate)) * up).astype(jnp.bfloat16)
+
+    for_live(at, e, run)
 
 
 def hidden_units(at, routed, w_gate, w_up, gate_in, up_in, e):
@@ -120,7 +133,7 @@
     half = w_gate.shape[2] // 2
     tile = min(TILE, half)
     return pl.pallas_call(
-        hidden_kernel,
+        functools.partial(hidden_kernel, e),
         grid_spec=pltpu.PrefetchScalarGridSpec(
             num_scalar_prefetch=1,
             grid=(half // tile,),
@@ -134,9 +147,14 @@
     )(at, routed, w_gate, w_up, gate_in, up_in)
 
 
-def down_kernel(at, own, other, own_matrix, other_matrix, weight, out):
-    summed = dot(own[...], own_matrix[0]) + dot(other[...], other_matrix[0])
-    out[...] = (summed * weight[...]).astype(jnp.bfloat16)
+def down_kernel(e, at, own, other, own_matrix, other_matrix, weight, out):
+    def run(rows):
+        summed = dot(own[:rows], own_matrix[0]) + dot(other[:rows], other_matrix[0])
+        out[:rows] = (summed * weight[:rows]).astype(jnp.bfloat16)
+        if rows < out.shape[0]:
+            out[rows:] = jnp.zeros((out.shape[0] - rows, out.shape[1]), out.dtype)
+
+    for_live(at, e, run)
 
 
 def weighted_down(at, own, other, w_down, weight, e):
@@ -144,7 +162,7 @@
     columns = w_down.shape[2]
     tile = min(TILE, columns)
     return pl.pallas_call(
-        down_kernel,
+        functools.partial(down_kernel, e),
         grid_spec=pltpu.PrefetchScalarGridSpec(
             num_scalar_prefetch=1,
             grid=(columns // tile,),
@@ -287,95 +305,104 @@
     )(tokens)
 
 
-def reduce_kernel(n, part, out, from_x, summed, from_z, final, x_send, x_recv, z_send, z_recv, f_send, f_recv):
+def reduce_kernel(n, pieces, part, out, from_x, summed, from_z, final, x_send, x_recv, z_send, z_recv, f_send, f_recv):
     x, z, r = lax.axis_index("expert"), lax.axis_index("tensor"), lax.axis_index("replica")
     per = n // 2
-    half, width = from_z.shape[1:]
+    half, width = pieces * from_z.shape[2], from_z.shape[3]
     meet(x, z, r, n)
 
-    def mine_of(side, block, core):
-        return part.at[rows_at(core * 2 * half + side * half, half), pl.ds(block * width, width)]
-
-    def x_copy(block, core):
-        return pltpu.make_async_remote_copy(
-            src_ref=mine_of(1 - x, block, core), dst_ref=from_x.at[block, core],
-            send_sem=x_send.at[block, core], recv_sem=x_recv.at[block, core],
+    size = half // pieces
+
+    def mine_of(side, p, block, core):
+        start = core * 2 * half + side * half + p * size
+        return part.at[rows_at(start, size), pl.ds(block * width, width)]
+
+    def x_copy(p, block, core):
+        return pltpu.make_async_remote_copy(
+            src_ref=mine_of(1 - x, p, block, core), dst_ref=from_x.at[p, block, core],
+            send_sem=x_send.at[p, block, core], recv_sem=x_recv.at[p, block, core],
             device_id={"expert": 1 - x}, device_id_type=MESH,
         )
 
-    def z_copy(block, core):
-        return pltpu.make_async_remote_copy(
-            src_ref=summed.at[block, core], dst_ref=from_z.at[z],
-            send_sem=z_send.at[block, core], recv_sem=z_recv.at[z],
+    def z_copy(p, block, core):
+        return pltpu.make_async_remote_copy(
+            src_ref=summed.at[p, block, core], dst_ref=from_z.at[p, z],
+            send_sem=z_send.at[p, block, core], recv_sem=z_recv.at[p, z],
             device_id={"tensor": per * r + block, "replica": core}, device_id_type=MESH,
         )
 
-    def arrival(source):
-        return pltpu.make_async_remote_copy(
-            src_ref=from_z.at[source], dst_ref=from_z.at[source],
-            send_sem=z_send.at[0, 0], recv_sem=z_recv.at[source],
+    def arrival(p, source):
+        return pltpu.make_async_remote_copy(
+            src_ref=from_z.at[p, source], dst_ref=from_z.at[p, source],
+            send_sem=z_send.at[p, 0, 0], recv_sem=z_recv.at[p, source],
             device_id={"expert": 1 - x}, device_id_type=MESH,
         )
 
-    def f_copy():
-        return pltpu.make_async_remote_copy(
-            src_ref=final.at[x], dst_ref=final.at[x], send_sem=f_send, recv_sem=f_recv,
+    def f_copy(p):
+        return pltpu.make_async_remote_copy(
+            src_ref=final.at[x, p], dst_ref=final.at[x, p], send_sem=f_send.at[p], recv_sem=f_recv.at[p],
             device_id={"expert": 1 - x}, device_id_type=MESH,
         )
 
-    places = [(block, core) for block in range(per) for core in range(2)]
+    places = [(p, block, core) for p in range(pieces) for block in range(per) for core in range(2)]
 
     def is_self(block, core):
         return (per * r + block == z) & (r == core)
 
-    for block, core in places:
-        x_copy(block, core).start()
-    for block, core in places:
-        x_copy(block, core).wait()
-        total = mine_of(x, block, core)[...].astype(jnp.float32) + from_x[block, core].astype(jnp.float32)
-        total = total.astype(jnp.bfloat16)
-        summed[block, core] = total
-
-        def keep(block=block, core=core):
-            from_z[z] = summed[block, core]
-
-        def send(block=block, core=core):
-            z_copy(block, core).start()
+    for p, block, core in places:
+        x_copy(p, block, core).start()
+    for p, block, core in places:
+        x_copy(p, block, core).wait()
+        total = mine_of(x, p, block, core)[...].astype(jnp.float32) + from_x[p, block, core].astype(jnp.float32)
+        summed[p, block, core] = total.astype(jnp.bfloat16)
+
+        def keep(p=p, block=block, core=core):
+            from_z[p, z] = summed[p, block, core]
+
+        def send(p=p, block=block, core=core):
+            z_copy(p, block, core).start()
 
         pl.when(is_self(block, core))(keep)
         pl.when(jnp.logical_not(is_self(block, core)))(send)
-    for source in range(n):
-        pl.when(jnp.logical_not((z == source) & (z // per == r)))(lambda source=source: arrival(source).wait_recv())
-    total = from_z[0].astype(jnp.float32)
-    for source in range(1, n):
-        total = total + from_z[source].astype(jnp.float32)
-    final[x] = total.astype(jnp.bfloat16)
-    f_copy().start()
-    for block, core in places:
+    for p in range(pieces):
+        for source in range(n):
+            pl.when(jnp.logical_not((z == source) & (z // per == r)))(
+                lambda p=p, source=source: arrival(p, source).wait_recv()
+            )
+        total = from_z[p, 0].astype(jnp.float32)
+        for source in range(1, n):
+            total = total + from_z[p, source].astype(jnp.float32)
+        final[x, p] = total.astype(jnp.bfloat16)
+        f_copy(p).start()
+    for p, block, core in places:
         pl.when(jnp.logical_not(is_self(block, core)))(
-            lambda block=block, core=core: z_copy(block, core).wait_send()
-        )
-    f_copy().wait()
+            lambda p=p, block=block, core=core: z_copy(p, block, core).wait_send()
+        )
+    for p in range(pieces):
+        f_copy(p).wait()
     for side in range(2):
-        out[pl.ds(side * half, half), :] = final[side]
+        for p in range(pieces):
+            out[pl.ds(side * half + p * size, size), :] = final[side, p]
 
 
 def reduce_parts(part, n):
     rows, columns = part.shape
     per = n // 2
-    half, width = rows // 4, columns // per
+    half, width, pieces = rows // 4, columns // per, 2
+    size = half // pieces
     dma, kind = pltpu.SemaphoreType.DMA, part.dtype
     return pl.pallas_call(
-        functools.partial(reduce_kernel, n),
+        functools.partial(reduce_kernel, n, pieces),
         out_shape=jax.ShapeDtypeStruct((rows // 2, width), kind),
         in_specs=[pl.BlockSpec(memory_space=pltpu.VMEM)],
         out_specs=pl.BlockSpec(memory_space=pltpu.VMEM),
         scratch_shapes=[
-            pltpu.VMEM((per, 2, half, width), kind),
-            pltpu.VMEM((per, 2, half, width), kind),
-            pltpu.VMEM((n, half, width), kind),
-            pltpu.VMEM((2, half, width), kind),
-            dma((per, 2)), dma((per, 2)), dma((per, 2)), dma((n,)), dma, dma,
+            pltpu.VMEM((pieces, per, 2, size, width), kind),
+            pltpu.VMEM((pieces, per, 2, size, width), kind),
+            pltpu.VMEM((pieces, n, size, width), kind),
+            pltpu.VMEM((2, pieces, size, width), kind),
+            dma((pieces, per, 2)), dma((pieces, per, 2)), dma((pieces, per, 2)), dma((pieces, n)),
+            dma((pieces,)), dma((pieces,)),
         ],
         compiler_params=compiler_params(collective_id=1, has_side_effects=True),
     )(part)
@@ -387,7 +414,7 @@
     experts = w_gate.shape[0]
     n_tensor = lax.axis_size("tensor")
     direct = lax.axis_size("expert") == 2 and n_tensor == 4
-    ids, weight = slot_lists(block_rows, block_gates, block_count, core, token_rows)
+    ids, weight, live = slot_lists(block_rows, block_gates, block_count, core, token_rows)
     if direct:
         table = gather_tokens(tokens, n_tensor)
     else:
@@ -398,7 +425,7 @@
             [jnp.where(core == 0, kept_rows, from_other), jnp.where(core == 0, from_other, kept_rows)], axis=0
         )
     token_at = jnp.arange(2 * token_rows, dtype=jnp.int32)
-    at = jnp.reshape(core, (1,)).astype(jnp.int32)
+    at = jnp.concatenate([jnp.reshape(core, (1,)).astype(jnp.int32), live])
 
     routed, sums = [], []
     for e in range(experts):

time: 202 us -> 187 us (0.926)
  Pallas kernels: 163 us -> 148 us
    pallas_call x7, Pallas kernels: 146 us -> 130 us  [the longest x1 52.8 us: reduce_parts(): pl.pallas_call(functools.partial(reduce_kernel, n, pieces), out_shape=jax...]
    unnamed x14 -> x16, local copies, waits for them, and re-layouts: 5.81 us -> 5.83 us
  transfers between devices with their start and end apart: 7 -> 7, of which waited for: 0 -> 0; matrix products, arithmetic and copies ran while one was open for 1% -> 1% of each run, Pallas kernels for 36% -> 37%
where the time goes in v2:
time: 187 us
  Pallas kernels  148 us (79%)
  starting transfers between devices  18.4 us (10%)
  matrix products  11.3 us (6%)
  local copies, waits for them, and re-layouts  6.49 us (3%)
  other arithmetic  2.61 us (1%)
    pallas_call x1, Pallas kernels, reduce_parts(): pl.pallas_call(functools.partial(reduce_kernel, n, pieces), out_shape=jax...  52.8 us
    pallas_call x2, Pallas kernels, weighted_down(): pl.pallas_call(functools.partial(down_kernel, e), grid_spec=pltpu.Prefetc...  26.2 us
    pallas_call x2, Pallas kernels, hidden_units(): pl.pallas_call(functools.partial(hidden_kernel, e), grid_spec=pltpu.Prefe...  26 us
    pallas_call x2, Pallas kernels, partial_sums(): pl.pallas_call(functools.partial(partial_kernel, e), grid_spec=pltpu.Pref...  25.4 us
    ppermute x7, starting transfers between devices, swap_cores(): return lax.ppermute(x, 'replica', SWAP)  18.4 us
    pallas_call x1, Pallas kernels, gather_tokens(): pl.pallas_call(functools.partial(gather_kernel, n, pieces), out_shape=jax...  17.3 us
    dot_general x3, matrix products, dot(): return jnp.dot(a, b, preferred_element_type=jnp.float32)  11.3 us
    unnamed x16, local copies, waits for them, and re-layouts  5.83 us
  transfers between devices with their start and end apart: 7, of which 0 were waited for; matrix products, arithmetic and copies ran while one was open for 1% of the time, Pallas kernels for 37%

profile of v2, /device:TPU:25, one launch (start us, length us, event | category | flops | bytes accessed | tf_op | source)
XLA Modules:
  0.0 186.8 jit_solution(10819390121936367424)
XLA Ops:
  0.0 0.7 convert_bitcast_fusion
  0.7 0.7 convert_element_type.56
  1.4 0.7 pad_maximum_fusion
  2.1 0.7 collective-permute-start
  2.9 1.1 copy-done.1
  4.0 17.3 %shard_map.73 = bf16[1024,1536]{1,0:T(8,128)(2,1)S(1)} custom-call(bf16[512,768]{1,0:T(8,128)(2,1)S(1)} %copy-done.1), custom_call_target="tpu_custom_call" | custom-call | tf_op jit(solution)/shard_map/pallas_call | solution.py:296
  22.0 3.0 %convolution_convert_fusion.routed = bf16[768,1536]{1,0:T(8,128)(2,1)S(1)} fusion(bf16[1024,1536]{1,0:T(8,128)(2,1)S(1)} %shard_map.73, s32[768]{0:T(1024)S(1)} %get-tuple-element.24), kind=kOutput, calls=%fused_computation.6 | convolution fusion | flops 2417885184 | bytes 5508096 | tf_op jit(solution)/shard_map/dot_general | solution.py:29
  25.0 3.0 %convolution_convert_fusion.1.routed = bf16[768,1536]{1,0:T(8,128)(2,1)S(1)} fusion(bf16[1024,1536]{1,0:T(8,128)(2,1)S(1)} %shard_map.73, s32[768]{0:T(1024)S(1)} %get-tuple-element.23), kind=kOutput, calls=%fused_computation.7 | convolution fusion | flops 2417885184 | bytes 5508096 | tf_op jit(solution)/shard_map/dot_general | solution.py:29
  28.0 11.3 %shard_map.74 = (bf16[768,2048]{1,0:T(8,128)(2,1)S(1)}, bf16[768,2048]{1,0:T(8,128)(2,1)}) custom-call(s32[3]{0:T(128)S(1)} %pad_add_fusion.at, bf16[768,1536]{1,0:T(8,128)(2,1)S(1)} %convolution_convert_fusion.1.routed, bf16[2,1536,4096]{2,1,0:T(8,128)(2,1)} %gate_matrix.7, bf16[2,1536,4096]{2,1,0:T(8,128)(2,1)} %up_matrix.7), custom_call_target="tpu_custom_call" | custom-call | flops 9663676416 | bytes 21233664 | tf_op jit(solution)/shard_map/pallas_call | solution.py:108
  39.2 16.6 %collective-permute-start.1 = (bf16[768,2048]{1,0:T(8,128)(2,1)S(1)}, bf16[768,2048]{1,0:T(8,128)(2,1)S(1)}, u32[]{:S(2)}, u32[]{:S(2)}) collective-permute-start(bf16[768,2048]{1,0:T(8,128)(2,1)S(1)} %get-tuple-element.9), channel_id=1, source_target_pairs={{0,1},{1,0},{2,3},{3,2},{4,5},{5,4},{6,7},{7,6},{8,9},{9,8},{10,11... | collective-permute-start | bytes 9437192 | tf_op jit(solution)/shard_map/ppermute | solution.py:20
  55.8 14.2 %shard_map.77 = (bf16[768,2048]{1,0:T(8,128)(2,1)S(1)}, bf16[768,2048]{1,0:T(8,128)(2,1)}) custom-call(s32[3]{0:T(128)S(1)} %pad_add_fusion.at, bf16[768,1536]{1,0:T(8,128)(2,1)S(1)} %convolution_convert_fusion.routed, bf16[2,1536,4096]{2,1,0:T(8,128)(2,1)} %gate_matrix.7, bf16[2,1536,4096]{2,1,0:T(8,128)(2,1)} %up_matrix.7), custom_call_target="tpu_custom_call" | custom-call | flops 9663676416 | bytes 21233664 | tf_op jit(solution)/shard_map/pallas_call | solution.py:108
  70.0 0.5 collective-permute-start.4
  70.5 1.7 copy-done.2
  72.2 11.2 %shard_map.75.own = bf16[768,2048]{1,0:T(8,128)(2,1)S(1)} custom-call(s32[3]{0:T(128)S(1)} %pad_add_fusion.at, bf16[768,1536]{1,0:T(8,128)(2,1)S(1)} %convolution_convert_fusion.1.routed, bf16[2,1536,4096]{2,1,0:T(8,128)(2,1)} %gate_matrix.7, bf16[2,1536,4096]{2,1,0:T(8,128)(2,1)} %up_matrix.7, bf16[768,2048]{1,0:T(8,128)(2,1)} %copy-done.2, ...), custom_call_target="tpu_custom_call" | custom-call | flops 9663676416 | bytes 21233664 | tf_op jit(solution)/shard_map/pallas_call | solution.py:135
  83.4 0.6 collective-permute-start.3
  83.9 14.8 %shard_map.78.own = bf16[768,2048]{1,0:T(8,128)(2,1)} custom-call(s32[3]{0:T(128)S(1)} %pad_add_fusion.at, bf16[768,1536]{1,0:T(8,128)(2,1)S(1)} %convolution_convert_fusion.routed, bf16[2,1536,4096]{2,1,0:T(8,128)(2,1)} %gate_matrix.7, bf16[2,1536,4096]{2,1,0:T(8,128)(2,1)} %up_matrix.7, bf16[768,2048]{1,0:T(8,128)(2,1)} %collective-permute-done.4.gate_in, ...), custom_call_target="tpu_custom_call" | custom-call | flops 9663676416 | bytes 21233664 | tf_op jit(solution)/shard_map/pallas_call | solution.py:135
  98.8 0.6 convert_element_type.63
  99.6 0.9 copy.13
  100.5 1.0 copy-done
  101.5 11.0 %shard_map.76 = bf16[768,1536]{1,0:T(8,128)(2,1)S(1)} custom-call(s32[3]{0:T(128)S(1)} %pad_add_fusion.at, bf16[768,2048]{1,0:T(8,128)(2,1)S(1)} %shard_map.75.own, bf16[768,2048]{1,0:T(8,128)(2,1)} %collective-permute-done.3.other, bf16[2,4096,1536]{2,1,0:T(8,128)(2,1)} %other_matrix.3, bf16[2,4096,1536]{2,1,0:T(8,128)(2,1)} %other_matrix.3, ...), custom_call_target="tpu_custom_call" | custom-call | flops 9663676416 | bytes 21233664 | tf_op jit(solution)/shard_map/pallas_call | solution.py:164
  112.6 15.2 %shard_map.79 = bf16[768,1536]{1,0:T(8,128)(2,1)S(1)} custom-call(s32[3]{0:T(128)S(1)} %pad_add_fusion.at, bf16[768,2048]{1,0:T(8,128)(2,1)} %shard_map.78.own, bf16[768,2048]{1,0:T(8,128)(2,1)} %collective-permute-done.6.other, bf16[2,4096,1536]{2,1,0:T(8,128)(2,1)} %other_matrix.3, bf16[2,4096,1536]{2,1,0:T(8,128)(2,1)} %other_matrix.3, f32[768,1]{1,0:T(8,128)S(1)} %bitcast.25), custom_call_target="tpu_custom_call" | custom-call | flops 9663676416 | bytes 21233664 | tf_op jit(solution)/shard_map/pallas_call | solution.py:164
  127.8 5.3 %fusion.4.part = bf16[1024,1536]{1,0:T(8,128)(2,1)S(1)} fusion(bf16[768,1536]{1,0:T(8,128)(2,1)S(1)} %shard_map.79, bf16[768,1536]{1,0:T(8,128)(2,1)S(1)} %shard_map.76, s32[1536]{0:T(1024)S(1)} %copy-done.4), kind=kOutput, calls=%fused_computation.5 | convolution fusion | flops 4844421120 | bytes 7870464 | tf_op jit(solution)/shard_map/dot_general | solution.py:29
  133.1 52.8 %shard_map.80 = bf16[512,768]{1,0:T(8,128)(2,1)S(1)} custom-call(bf16[1024,1536]{1,0:T(8,128)(2,1)S(1)} %fusion.4.part), custom_call_target="tpu_custom_call" | custom-call | tf_op jit(solution)/shard_map/pallas_call | solution.py:394
  185.9 0.9 copy.21
  (35 shorter events, 0.9 us)
Async XLA Ops:
  0.0 21.3 %copy-start.3 = (f32[2,1,512]{2,1,0:T(1,128)S(1)}, f32[2,1,512]{2,1,0:T(1,128)}, u32[]{:S(2)}) copy-start(f32[2,1,512]{2,1,0:T(1,128)} %param.12) | copy-start | bytes 12292
  2.1 19.2 %collective-permute-start = (f32[2,3,512]{2,1,0:T(4,128)S(1)}, f32[2,3,512]{2,1,0:T(4,128)S(1)}, u32[]{:S(2)}, u32[]{:S(2)}) collective-permute-start(f32[2,3,512]{2,1,0:T(4,128)S(1)} %pad_maximum_fusion), channel_id=1, source_target_pairs={{0,1},{1,0},{2,3},{3,2},{4,5},{5,4},{6,7},{7,6},{8,9},{9,8},{10,11... | collective-permute-start | bytes 36872 | tf_op jit(solution)/shard_map/ppermute | solution.py:20
  2.9 1.1 copy-start.1
  39.2 31.3 %collective-permute-start.1 = (bf16[768,2048]{1,0:T(8,128)(2,1)S(1)}, bf16[768,2048]{1,0:T(8,128)(2,1)S(1)}, u32[]{:S(2)}, u32[]{:S(2)}) collective-permute-start(bf16[768,2048]{1,0:T(8,128)(2,1)S(1)} %get-tuple-element.9), channel_id=1, source_target_pairs={{0,1},{1,0},{2,3},{3,2},{4,5},{5,4},{6,7},{7,6},{8,9},{9,8},{10,11... | collective-permute-start | bytes 9437192 | tf_op jit(solution)/shard_map/ppermute | solution.py:20
  55.8 16.4 %collective-permute-start.2 = (bf16[768,2048]{1,0:T(8,128)(2,1)}, bf16[768,2048]{1,0:T(8,128)(2,1)}, u32[]{:S(2)}, u32[]{:S(2)}) collective-permute-start(bf16[768,2048]{1,0:T(8,128)(2,1)} %get-tuple-element.10), channel_id=1, source_target_pairs={{0,1},{1,0},{2,3},{3,2},{4,5},{5,4},{6,7},{7,6},{8,9},{9,8},{10,11... | collective-permute-start | bytes 9437192 | tf_op jit(solution)/shard_map/ppermute | solution.py:20
  70.0 13.9 %collective-permute-start.4 = (bf16[768,2048]{1,0:T(8,128)(2,1)S(1)}, bf16[768,2048]{1,0:T(8,128)(2,1)}, u32[]{:S(2)}, u32[]{:S(2)}) collective-permute-start(bf16[768,2048]{1,0:T(8,128)(2,1)S(1)} %get-tuple-element.11), channel_id=1, source_target_pairs={{0,1},{1,0},{2,3},{3,2},{4,5},{5,4},{6,7},{7,6},{8,9},{9,8},{10,11... | collective-permute-start | bytes 9437192 | tf_op jit(solution)/shard_map/ppermute | solution.py:20
  70.5 13.4 %collective-permute-start.5 = (bf16[768,2048]{1,0:T(8,128)(2,1)}, bf16[768,2048]{1,0:T(8,128)(2,1)}, u32[]{:S(2)}, u32[]{:S(2)}) collective-permute-start(bf16[768,2048]{1,0:T(8,128)(2,1)} %get-tuple-element.12), channel_id=1, source_target_pairs={{0,1},{1,0},{2,3},{3,2},{4,5},{5,4},{6,7},{7,6},{8,9},{9,8},{10,11... | collective-permute-start | bytes 9437192 | tf_op jit(solution)/shard_map/ppermute | solution.py:20
  70.5 1.7 copy-start.2
  83.4 17.2 %collective-permute-start.3 = (bf16[768,2048]{1,0:T(8,128)(2,1)S(1)}, bf16[768,2048]{1,0:T(8,128)(2,1)}, u32[]{:S(2)}, u32[]{:S(2)}) collective-permute-start(bf16[768,2048]{1,0:T(8,128)(2,1)S(1)} %shard_map.75.own), channel_id=1, source_target_pairs={{0,1},{1,0},{2,3},{3,2},{4,5},{5,4},{6,7},{7,6},{8,9},{9,8},{10,11... | collective-permute-start | bytes 9437192 | tf_op jit(solution)/shard_map/ppermute | solution.py:20
  98.8 13.8 %collective-permute-start.6 = (bf16[768,2048]{1,0:T(8,128)(2,1)}, bf16[768,2048]{1,0:T(8,128)(2,1)}, u32[]{:S(2)}, u32[]{:S(2)}) collective-permute-start(bf16[768,2048]{1,0:T(8,128)(2,1)} %shard_map.78.own), channel_id=1, source_target_pairs={{0,1},{1,0},{2,3},{3,2},{4,5},{5,4},{6,7},{7,6},{8,9},{9,8},{10,11... | collective-permute-start | bytes 9437192 | tf_op jit(solution)/shard_map/ppermute | solution.py:20
  100.5 1.0 copy-start
  112.6 15.2 %copy-start.4 = (s32[1536]{0:T(1024)S(1)}, s32[1536]{0:T(1024)}, u32[]{:S(2)}) copy-start(s32[1536]{0:T(1024)} %convert_element_type.63) | copy-start | bytes 18436
